TPU v7x, 256 devices: a whole 4x4x8 slice. The times are simulated.
256 devices in a mesh: blk: 16 (over z, y_lo), grp: 16 (over x, y_hi, core).
Axes of the slice: x: 4, y: 4 (y_hi: 2, y_lo: 2; y = y_hi * 2 + y_lo), z: 8, core: 2. Of those that a mesh axis runs over, the one named last changes fastest.
Arguments:
- state: float32 [2, 128, 32768], P(None, None, ('blk', 'grp')), may hold values from -3 to 3
- prev_slope: float32 [2, 128, 32768], P(None, None, ('blk', 'grp')), may hold values from -4 to 4
- positions: float32 [2, 32768], P(None, ('blk', 'grp')), may hold values from -1 to 1
- pump: float32 [32768], P(('blk', 'grp')), may hold values from -0.5 to 1.5
- detuning: float32 [32768], P(('blk', 'grp')), may hold values from -4 to 4
- kappa: float32 [6, 32768], P(None, ('blk', 'grp')), may hold values from 0.2 to 1
- neighbours: int32 [6, 32768], P(None, ('blk', 'grp')), may hold values from 0 to 255
- send_list: int32 [2, 16384], P(None, ('blk', 'grp')), may hold values from 0 to 127
Outputs:
- slope: float32 [2, 128, 32768], P(None, None, ('blk', 'grp'))
Inputs may be any that keep to these rules, and one draw needn't show every extreme that they name: `neighbours`: places below 128 are the block's own emitters, the next 64 those listed by the previous block, the last 64 those listed by the next block. `send_list`: places in the listing block.
All inputs are finite; a program needn't handle non-finite values.
Results may differ from a plain program's by a relative error of at most 0.0012.
Values may be sent and summed in bfloat16 or wider, within the bound.
A program may use at most 64 MiB of HBM per device.

v0:
```python
import math
import jax
import jax.numpy as jnp
from jax import lax
from jax.sharding import PartitionSpec as P

section_weight = 0.25
phase_rate = 60.0
alpha_factor = 2.0


def from_behind(array, axis, by):
    size = lax.axis_size(axis)
    return lax.ppermute(array, axis, [(i, (i + by) % size) for i in range(size)])


def with_halo(cells, sides, width):
    for axis, dim in sides:
        count = lax.axis_size(axis)
        ends = count - 1
        head = lax.slice_in_dim(cells, 0, width, axis=dim)
        tail = lax.slice_in_dim(cells, cells.shape[dim] - width, cells.shape[dim], axis=dim)
        cells = jnp.concatenate(
            [
                lax.ppermute(tail, axis, [(i, (i + 1) % count) for i in range(ends)]),
                cells,
                lax.ppermute(head, axis, [((i + 1) % count, i) for i in range(ends)]),
            ],
            axis=dim,
        )
    return cells


def kernel_table(source_place, target_place, scaled):
    horizontal = target_place[0][None, :] - source_place[0][:, None]
    vertical = target_place[1][None, :] - source_place[1][:, None]
    phase = phase_rate * (horizontal * horizontal + vertical * vertical)
    cosine = (scaled * jnp.cos(phase)).astype(jnp.bfloat16)
    sine_part = (scaled * jnp.sin(phase)).astype(jnp.bfloat16)
    return jnp.concatenate([cosine, sine_part], axis=1)


def block_columns(total, fields, source_place, target_place, scaled):
    members = fields.shape[1]
    targets = target_place.shape[1]
    kernel = kernel_table(source_place, target_place, scaled)
    flat = fields.reshape(2 * members, fields.shape[2])
    product = jnp.dot(flat, kernel, preferred_element_type=jnp.float32)
    real_part = product[:members, :targets] - product[members:, targets:]
    imag_part = product[:members, targets:] + product[members:, :targets]
    return total + jnp.stack([real_part, imag_part])


def local(state, prev_slope, positions, pump, detuning, kappa, neighbours, send_list):
    members = state.shape[1]
    rows_here = state.shape[2]
    block_count = lax.axis_size("blk")
    group_size = lax.axis_size("grp")
    scaled = 1.0 / math.sqrt(rows_here * block_count * group_size)
    section_field = state + section_weight * prev_slope
    section_half = section_field.astype(jnp.bfloat16)
    my_index = lax.axis_index("blk")
    target_place = lax.all_gather(positions, "grp", axis=1, tiled=True)
    source_place = lax.all_gather(positions, "blk", axis=1, tiled=True)
    targets = target_place.shape[1]

    def place_of(block_index):
        return lax.dynamic_slice_in_dim(
            source_place, block_index % block_count * rows_here, rows_here, 1
        )

    def add_block(total, fields, block_index):
        return block_columns(total, fields, place_of(block_index), target_place, scaled)

    empty = jnp.zeros((2, members, targets), jnp.float32)

    def advance(step, carry):
        total, carried = carry
        carried = from_behind(carried, "blk", 1)
        return (add_block(total, carried, my_index - step), carried)

    total = add_block(empty, section_half, my_index)
    total, carried = lax.fori_loop(1, block_count, advance, (total, section_half))
    fresnel = lax.psum_scatter(total, "grp", scatter_dimension=2, tiled=True)
    halo_width = send_list.shape[1]
    to_prev = jnp.take(section_field, send_list[1], axis=2)
    to_next = jnp.take(section_field, send_list[0], axis=2)
    padded = with_halo(
        jnp.concatenate([to_prev, to_next], axis=2), ((("blk", "grp"), 2),), halo_width
    )
    local_buffer = jnp.concatenate(
        [section_field, padded[:, :, :halo_width], padded[:, :, 3 * halo_width :]], axis=2
    )
    coupled = jnp.zeros((2, members, rows_here), jnp.float32)
    for neighbour_slot in range(kappa.shape[0]):
        picked = jnp.take(local_buffer, neighbours[neighbour_slot], axis=2)
        coupled = coupled + kappa[neighbour_slot] * picked
    real_field = section_field[0]
    imag_field = section_field[1]
    modulus = real_field * real_field + imag_field * imag_field
    linear_real = pump - modulus
    linear_imag = detuning - alpha_factor * modulus
    local_real = linear_real * real_field - linear_imag * imag_field
    local_imag = linear_real * imag_field + linear_imag * real_field
    slope_real = local_real + fresnel[0] - coupled[1]
    slope_imag = local_imag + fresnel[1] + coupled[0]
    return jnp.stack([slope_real, slope_imag])


def solution(mesh):
    placed = (
        P(None, None, ("blk", "grp")),
        P(None, None, ("blk", "grp")),
        P(None, ("blk", "grp")),
        P(("blk", "grp")),
        P(("blk", "grp")),
        P(None, ("blk", "grp")),
        P(None, ("blk", "grp")),
        P(None, ("blk", "grp")),
    )
    return jax.shard_map(
        local, mesh=mesh, in_specs=placed, out_specs=P(None, None, ("blk", "grp")), check_vma=False
    )
```

profile of v0, /device:TPU:1, one launch (start us, length us, event | category | flops | bytes accessed | tf_op | source)
XLA Modules:
  0.0 357.1 jit_solution(1901654275807691150)
XLA Ops:
  6.5 30.5 %all_gather.7 = f32[2,2048]{1,0:T(2,128)S(1)} all-gather(f32[2,128]{1,0:T(2,128)} %param.16), channel_id=1, replica_groups=mesh['blk'=16,'grp'=16] {'blk'}, dimensions={1}, use_global_device_ids=true | all-gather | bytes 17408 | tf_op jit(solution)/shard_map/all_gather | solution.py:64
  37.1 31.7 %all_gather.6 = f32[2,2048]{1,0:T(2,128)S(1)} all-gather(f32[2,128]{1,0:T(2,128)} %param.16), channel_id=1, replica_groups=mesh['blk'=16,'grp'=16] {'grp'}, dimensions={1}, use_global_device_ids=true | all-gather | bytes 17408 | tf_op jit(solution)/shard_map/all_gather | solution.py:63
  68.8 1.0 fusion.18
  69.8 4.3 %multiply_convert_fusion.3 = (bf16[128,2048]{1,0:T(8,128)(2,1)S(1)}, bf16[128,2048]{1,0:T(8,128)(2,1)S(1)}) fusion(f32[128]{0:T(128)S(1)} %get-tuple-element.252, f32[2048]{0:T(1024)S(1)} %bitcast.118, f32[128]{0:T(128)S(1)} %get-tuple-element.251, f32[2048]{0:T(1024)S(1)} %bitcast.117), kind=kLoop, calls=%fused_computation.34 | loop fusion | flops 2621440 | bytes 1065984 | tf_op jit(solution)/shard_map/convert_element_type | solution.py:38
  74.1 0.7 fusion.8
  75.1 1.5 pad_maximum_fusion
  76.6 1.9 copy.23
  78.5 102.8 %while.17 = (s32[]{:T(128)}, f32[2,128,2048]{1,2,0:T(8,128)S(1)}, bf16[2,128,128]{2,1,0:T(8,128)(2,1)S(1)}, f32[2,2048]{1,0:T(2,128)S(1)}, s32[]{:T(128)}, /*ind...) while((s32[]{:T(128)}, f32[2,128,2048]{1,2,0:T(8,128)S(1)}, ...), condition=%wide.region_1.2_spmd, body=%wide.region_0.1_spmd.sunk | while | flops 274726944 | bytes 19387720 | solution.py:83
  78.7 4.3 %multiply_convert_fusion.5 = (bf16[128,2048]{1,0:T(8,128)(2,1)S(1)}, bf16[128,2048]{1,0:T(8,128)(2,1)S(1)}) fusion(f32[128]{0:T(128)S(1)} %get-tuple-element.306, f32[2048]{0:T(1024)S(1)} %bitcast.115, f32[128]{0:T(128)S(1)} %get-tuple-element.308, f32[2048]{0:T(1024)S(1)} %bitcast.114), kind=kLoop, calls=%fused_computation.18.clone.1 | loop fusion | flops 2621440 | bytes 1065984 | tf_op jit(solution)/shard_map/while/body/eval_jaxpr/convert_element_type | solution.py:38
  83.0 1.2 collective-permute-done
  84.2 0.7 convolution_bitcast_fusion.2
  85.8 4.3 %multiply_convert_fusion.5 = (bf16[128,2048]{1,0:T(8,128)(2,1)S(1)}, bf16[128,2048]{1,0:T(8,128)(2,1)S(1)}) fusion(f32[128]{0:T(128)S(1)} %get-tuple-element.306, f32[2048]{0:T(1024)S(1)} %bitcast.115, f32[128]{0:T(128)S(1)} %get-tuple-element.308, f32[2048]{0:T(1024)S(1)} %bitcast.114), kind=kLoop, calls=%fused_computation.18.clone.1 | loop fusion | flops 2621440 | bytes 1065984 | tf_op jit(solution)/shard_map/while/body/eval_jaxpr/convert_element_type | solution.py:38
  90.1 0.8 collective-permute-done
  90.9 0.7 convolution_bitcast_fusion.2
  92.6 4.3 %multiply_convert_fusion.5 = (bf16[128,2048]{1,0:T(8,128)(2,1)S(1)}, bf16[128,2048]{1,0:T(8,128)(2,1)S(1)}) fusion(f32[128]{0:T(128)S(1)} %get-tuple-element.306, f32[2048]{0:T(1024)S(1)} %bitcast.115, f32[128]{0:T(128)S(1)} %get-tuple-element.308, f32[2048]{0:T(1024)S(1)} %bitcast.114), kind=kLoop, calls=%fused_computation.18.clone.1 | loop fusion | flops 2621440 | bytes 1065984 | tf_op jit(solution)/shard_map/while/body/eval_jaxpr/convert_element_type | solution.py:38
  96.8 0.8 collective-permute-done
  97.7 0.7 convolution_bitcast_fusion.2
  99.3 4.3 %multiply_convert_fusion.5 = (bf16[128,2048]{1,0:T(8,128)(2,1)S(1)}, bf16[128,2048]{1,0:T(8,128)(2,1)S(1)}) fusion(f32[128]{0:T(128)S(1)} %get-tuple-element.306, f32[2048]{0:T(1024)S(1)} %bitcast.115, f32[128]{0:T(128)S(1)} %get-tuple-element.308, f32[2048]{0:T(1024)S(1)} %bitcast.114), kind=kLoop, calls=%fused_computation.18.clone.1 | loop fusion | flops 2621440 | bytes 1065984 | tf_op jit(solution)/shard_map/while/body/eval_jaxpr/convert_element_type | solution.py:38
  103.6 0.8 collective-permute-done
  104.4 0.7 convolution_bitcast_fusion.2
  106.0 4.3 %multiply_convert_fusion.5 = (bf16[128,2048]{1,0:T(8,128)(2,1)S(1)}, bf16[128,2048]{1,0:T(8,128)(2,1)S(1)}) fusion(f32[128]{0:T(128)S(1)} %get-tuple-element.306, f32[2048]{0:T(1024)S(1)} %bitcast.115, f32[128]{0:T(128)S(1)} %get-tuple-element.308, f32[2048]{0:T(1024)S(1)} %bitcast.114), kind=kLoop, calls=%fused_computation.18.clone.1 | loop fusion | flops 2621440 | bytes 1065984 | tf_op jit(solution)/shard_map/while/body/eval_jaxpr/convert_element_type | solution.py:38
  110.3 0.8 collective-permute-done
  111.2 0.7 convolution_bitcast_fusion.2
  112.8 4.3 %multiply_convert_fusion.5 = (bf16[128,2048]{1,0:T(8,128)(2,1)S(1)}, bf16[128,2048]{1,0:T(8,128)(2,1)S(1)}) fusion(f32[128]{0:T(128)S(1)} %get-tuple-element.306, f32[2048]{0:T(1024)S(1)} %bitcast.115, f32[128]{0:T(128)S(1)} %get-tuple-element.308, f32[2048]{0:T(1024)S(1)} %bitcast.114), kind=kLoop, calls=%fused_computation.18.clone.1 | loop fusion | flops 2621440 | bytes 1065984 | tf_op jit(solution)/shard_map/while/body/eval_jaxpr/convert_element_type | solution.py:38
  117.1 0.8 collective-permute-done
  117.9 0.7 convolution_bitcast_fusion.2
  119.5 4.3 %multiply_convert_fusion.5 = (bf16[128,2048]{1,0:T(8,128)(2,1)S(1)}, bf16[128,2048]{1,0:T(8,128)(2,1)S(1)}) fusion(f32[128]{0:T(128)S(1)} %get-tuple-element.306, f32[2048]{0:T(1024)S(1)} %bitcast.115, f32[128]{0:T(128)S(1)} %get-tuple-element.308, f32[2048]{0:T(1024)S(1)} %bitcast.114), kind=kLoop, calls=%fused_computation.18.clone.1 | loop fusion | flops 2621440 | bytes 1065984 | tf_op jit(solution)/shard_map/while/body/eval_jaxpr/convert_element_type | solution.py:38
  123.8 0.9 collective-permute-done
  124.7 0.7 convolution_bitcast_fusion.2
  126.1 0.6 collective-permute-start
  126.7 4.3 %multiply_convert_fusion.5 = (bf16[128,2048]{1,0:T(8,128)(2,1)S(1)}, bf16[128,2048]{1,0:T(8,128)(2,1)S(1)}) fusion(f32[128]{0:T(128)S(1)} %get-tuple-element.306, f32[2048]{0:T(1024)S(1)} %bitcast.115, f32[128]{0:T(128)S(1)} %get-tuple-element.308, f32[2048]{0:T(1024)S(1)} %bitcast.114), kind=kLoop, calls=%fused_computation.18.clone.1 | loop fusion | flops 2621440 | bytes 1065984 | tf_op jit(solution)/shard_map/while/body/eval_jaxpr/convert_element_type | solution.py:38
  131.0 1.0 collective-permute-done
  132.0 0.7 convolution_bitcast_fusion.2
  133.9 4.3 %multiply_convert_fusion.5 = (bf16[128,2048]{1,0:T(8,128)(2,1)S(1)}, bf16[128,2048]{1,0:T(8,128)(2,1)S(1)}) fusion(f32[128]{0:T(128)S(1)} %get-tuple-element.306, f32[2048]{0:T(1024)S(1)} %bitcast.115, f32[128]{0:T(128)S(1)} %get-tuple-element.308, f32[2048]{0:T(1024)S(1)} %bitcast.114), kind=kLoop, calls=%fused_computation.18.clone.1 | loop fusion | flops 2621440 | bytes 1065984 | tf_op jit(solution)/shard_map/while/body/eval_jaxpr/convert_element_type | solution.py:38
  138.7 0.7 convolution_bitcast_fusion.2
  140.6 4.3 %multiply_convert_fusion.5 = (bf16[128,2048]{1,0:T(8,128)(2,1)S(1)}, bf16[128,2048]{1,0:T(8,128)(2,1)S(1)}) fusion(f32[128]{0:T(128)S(1)} %get-tuple-element.306, f32[2048]{0:T(1024)S(1)} %bitcast.115, f32[128]{0:T(128)S(1)} %get-tuple-element.308, f32[2048]{0:T(1024)S(1)} %bitcast.114), kind=kLoop, calls=%fused_computation.18.clone.1 | loop fusion | flops 2621440 | bytes 1065984 | tf_op jit(solution)/shard_map/while/body/eval_jaxpr/convert_element_type | solution.py:38
  145.5 0.7 convolution_bitcast_fusion.2
  147.4 4.3 %multiply_convert_fusion.5 = (bf16[128,2048]{1,0:T(8,128)(2,1)S(1)}, bf16[128,2048]{1,0:T(8,128)(2,1)S(1)}) fusion(f32[128]{0:T(128)S(1)} %get-tuple-element.306, f32[2048]{0:T(1024)S(1)} %bitcast.115, f32[128]{0:T(128)S(1)} %get-tuple-element.308, f32[2048]{0:T(1024)S(1)} %bitcast.114), kind=kLoop, calls=%fused_computation.18.clone.1 | loop fusion | flops 2621440 | bytes 1065984 | tf_op jit(solution)/shard_map/while/body/eval_jaxpr/convert_element_type | solution.py:38
  152.2 0.7 convolution_bitcast_fusion.2
  154.1 4.3 %multiply_convert_fusion.5 = (bf16[128,2048]{1,0:T(8,128)(2,1)S(1)}, bf16[128,2048]{1,0:T(8,128)(2,1)S(1)}) fusion(f32[128]{0:T(128)S(1)} %get-tuple-element.306, f32[2048]{0:T(1024)S(1)} %bitcast.115, f32[128]{0:T(128)S(1)} %get-tuple-element.308, f32[2048]{0:T(1024)S(1)} %bitcast.114), kind=kLoop, calls=%fused_computation.18.clone.1 | loop fusion | flops 2621440 | bytes 1065984 | tf_op jit(solution)/shard_map/while/body/eval_jaxpr/convert_element_type | solution.py:38
  159.0 0.7 convolution_bitcast_fusion.2
  160.9 4.3 %multiply_convert_fusion.5 = (bf16[128,2048]{1,0:T(8,128)(2,1)S(1)}, bf16[128,2048]{1,0:T(8,128)(2,1)S(1)}) fusion(f32[128]{0:T(128)S(1)} %get-tuple-element.306, f32[2048]{0:T(1024)S(1)} %bitcast.115, f32[128]{0:T(128)S(1)} %get-tuple-element.308, f32[2048]{0:T(1024)S(1)} %bitcast.114), kind=kLoop, calls=%fused_computation.18.clone.1 | loop fusion | flops 2621440 | bytes 1065984 | tf_op jit(solution)/shard_map/while/body/eval_jaxpr/convert_element_type | solution.py:38
  165.7 0.7 convolution_bitcast_fusion.2
  167.6 4.3 %multiply_convert_fusion.5 = (bf16[128,2048]{1,0:T(8,128)(2,1)S(1)}, bf16[128,2048]{1,0:T(8,128)(2,1)S(1)}) fusion(f32[128]{0:T(128)S(1)} %get-tuple-element.306, f32[2048]{0:T(1024)S(1)} %bitcast.115, f32[128]{0:T(128)S(1)} %get-tuple-element.308, f32[2048]{0:T(1024)S(1)} %bitcast.114), kind=kLoop, calls=%fused_computation.18.clone.1 | loop fusion | flops 2621440 | bytes 1065984 | tf_op jit(solution)/shard_map/while/body/eval_jaxpr/convert_element_type | solution.py:38
  172.5 0.7 convolution_bitcast_fusion.2
  174.4 4.3 %multiply_convert_fusion.5 = (bf16[128,2048]{1,0:T(8,128)(2,1)S(1)}, bf16[128,2048]{1,0:T(8,128)(2,1)S(1)}) fusion(f32[128]{0:T(128)S(1)} %get-tuple-element.306, f32[2048]{0:T(1024)S(1)} %bitcast.115, f32[128]{0:T(128)S(1)} %get-tuple-element.308, f32[2048]{0:T(1024)S(1)} %bitcast.114), kind=kLoop, calls=%fused_computation.18.clone.1 | loop fusion | flops 2621440 | bytes 1065984 | tf_op jit(solution)/shard_map/while/body/eval_jaxpr/convert_element_type | solution.py:38
  178.7 1.2 collective-permute-done
  179.9 0.7 convolution_bitcast_fusion.2
  181.3 8.5 %copy.24 = f32[2,128,2048]{1,0,2:T(2,128)} copy(f32[2,128,2048]{1,2,0:T(8,128)S(1)} %get-tuple-element.162) | data formatting | bytes 4194304 | tf_op jit(solution)/shard_map/while | solution.py:83
  190.6 0.7 gather_fusion
  191.3 16.5 %collective-permute-start.1 = (f32[2,128,64]{2,1,0:T(8,128)S(1)}, f32[2,128,64]{2,1,0:T(8,128)S(1)}, u32[]{:S(2)}, u32[]{:S(2)}) collective-permute-start(f32[2,128,64]{2,1,0:T(8,128)S(1)} %select_bitcast_fusion.1), channel_id=1, source_target_pairs={{0,1},{1,2},{2,3},{3,4},{4,5},{5,6},{6,7},{7,8},{8,9},{9,10},{10,1... | collective-permute-start | bytes 196616 | tf_op jit(solution)/shard_map/ppermute | solution.py:25
  207.9 0.7 gather_fusion.1
  208.7 3.2 collective-permute-start.2
  211.9 0.6 dynamic-slice
  213.2 5.7 %collective-permute-done.2 = f32[2,128,64]{2,1,0:T(8,128)S(1)} collective-permute-done((f32[2,128,64]{2,1,0:T(8,128)S(1)}, f32[2,128,64]{2,1,0:T(8,128)S(1)}, u32[]{:S(2)}, u32[]{:S(2)}) %collective-permute-start.2) | collective-permute-done | bytes 65568 | tf_op jit(solution)/shard_map/ppermute | solution.py:27
  219.2 0.7 gather_fusion.2
  220.0 0.7 gather_fusion.3
  220.9 0.7 gather_fusion.4
  221.7 0.7 gather_fusion.5
  222.6 0.7 gather_fusion.6
  223.5 0.8 gather_fusion.7
  224.4 123.8 %all-reduce.3.cloned.1.call-done = f32[2,128,2048]{1,0,2:T(2,128)} async-done(((f32[2,128,2048]{1,0,2:T(2,128)}), f32[2,128,2048]{1,0,2:T(2,128)}) %all-reduce.3.cloned.1.call-update) | async-done | bytes 2097168
  348.2 1.1 constant_dynamic-slice_fusion.1
  349.6 0.7 pad_maximum_fusion.2
  (154 shorter events, 19.8 us)
Async XLA Ops:
  6.5 341.7 %all-reduce.3.cloned.1.call-start = ((), (), s32[]{:S(2)}) async-start(), calls=%async_computation | async-start | bytes 4194304
  78.5 5.7 %collective-permute-start = (bf16[2,128,128]{2,1,0:T(8,128)(2,1)S(1)}, bf16[2,128,128]{2,1,0:T(8,128)(2,1)S(1)}, u32[]{:S(2)}, u32[]{:S(2)}) collective-permute-start(bf16[2,128,128]{2,1,0:T(8,128)(2,1)S(1)} %get-tuple-element.328), channel_id=1, source_target_pairs={{0,16},{16,32},{32,48},{48,64},{64,80},{80,96},{96,112},{112,128},... | collective-permute-start | bytes 196616 | tf_op jit(solution)/shard_map/while/body/eval_jaxpr/ppermute | solution.py:14
  85.6 5.3 %collective-permute-start = (bf16[2,128,128]{2,1,0:T(8,128)(2,1)S(1)}, bf16[2,128,128]{2,1,0:T(8,128)(2,1)S(1)}, u32[]{:S(2)}, u32[]{:S(2)}) collective-permute-start(bf16[2,128,128]{2,1,0:T(8,128)(2,1)S(1)} %get-tuple-element.328), channel_id=1, source_target_pairs={{0,16},{16,32},{32,48},{48,64},{64,80},{80,96},{96,112},{112,128},... | collective-permute-start | bytes 196616 | tf_op jit(solution)/shard_map/while/body/eval_jaxpr/ppermute | solution.py:14
  92.4 5.3 %collective-permute-start = (bf16[2,128,128]{2,1,0:T(8,128)(2,1)S(1)}, bf16[2,128,128]{2,1,0:T(8,128)(2,1)S(1)}, u32[]{:S(2)}, u32[]{:S(2)}) collective-permute-start(bf16[2,128,128]{2,1,0:T(8,128)(2,1)S(1)} %get-tuple-element.328), channel_id=1, source_target_pairs={{0,16},{16,32},{32,48},{48,64},{64,80},{80,96},{96,112},{112,128},... | collective-permute-start | bytes 196616 | tf_op jit(solution)/shard_map/while/body/eval_jaxpr/ppermute | solution.py:14
  99.1 5.3 %collective-permute-start = (bf16[2,128,128]{2,1,0:T(8,128)(2,1)S(1)}, bf16[2,128,128]{2,1,0:T(8,128)(2,1)S(1)}, u32[]{:S(2)}, u32[]{:S(2)}) collective-permute-start(bf16[2,128,128]{2,1,0:T(8,128)(2,1)S(1)} %get-tuple-element.328), channel_id=1, source_target_pairs={{0,16},{16,32},{32,48},{48,64},{64,80},{80,96},{96,112},{112,128},... | collective-permute-start | bytes 196616 | tf_op jit(solution)/shard_map/while/body/eval_jaxpr/ppermute | solution.py:14
  105.9 5.3 %collective-permute-start = (bf16[2,128,128]{2,1,0:T(8,128)(2,1)S(1)}, bf16[2,128,128]{2,1,0:T(8,128)(2,1)S(1)}, u32[]{:S(2)}, u32[]{:S(2)}) collective-permute-start(bf16[2,128,128]{2,1,0:T(8,128)(2,1)S(1)} %get-tuple-element.328), channel_id=1, source_target_pairs={{0,16},{16,32},{32,48},{48,64},{64,80},{80,96},{96,112},{112,128},... | collective-permute-start | bytes 196616 | tf_op jit(solution)/shard_map/while/body/eval_jaxpr/ppermute | solution.py:14
  112.6 5.3 %collective-permute-start = (bf16[2,128,128]{2,1,0:T(8,128)(2,1)S(1)}, bf16[2,128,128]{2,1,0:T(8,128)(2,1)S(1)}, u32[]{:S(2)}, u32[]{:S(2)}) collective-permute-start(bf16[2,128,128]{2,1,0:T(8,128)(2,1)S(1)} %get-tuple-element.328), channel_id=1, source_target_pairs={{0,16},{16,32},{32,48},{48,64},{64,80},{80,96},{96,112},{112,128},... | collective-permute-start | bytes 196616 | tf_op jit(solution)/shard_map/while/body/eval_jaxpr/ppermute | solution.py:14
  119.4 5.3 %collective-permute-start = (bf16[2,128,128]{2,1,0:T(8,128)(2,1)S(1)}, bf16[2,128,128]{2,1,0:T(8,128)(2,1)S(1)}, u32[]{:S(2)}, u32[]{:S(2)}) collective-permute-start(bf16[2,128,128]{2,1,0:T(8,128)(2,1)S(1)} %get-tuple-element.328), channel_id=1, source_target_pairs={{0,16},{16,32},{32,48},{48,64},{64,80},{80,96},{96,112},{112,128},... | collective-permute-start | bytes 196616 | tf_op jit(solution)/shard_map/while/body/eval_jaxpr/ppermute | solution.py:14
  126.1 5.8 %collective-permute-start = (bf16[2,128,128]{2,1,0:T(8,128)(2,1)S(1)}, bf16[2,128,128]{2,1,0:T(8,128)(2,1)S(1)}, u32[]{:S(2)}, u32[]{:S(2)}) collective-permute-start(bf16[2,128,128]{2,1,0:T(8,128)(2,1)S(1)} %get-tuple-element.328), channel_id=1, source_target_pairs={{0,16},{16,32},{32,48},{48,64},{64,80},{80,96},{96,112},{112,128},... | collective-permute-start | bytes 196616 | tf_op jit(solution)/shard_map/while/body/eval_jaxpr/ppermute | solution.py:14
  133.4 5.3 %collective-permute-start = (bf16[2,128,128]{2,1,0:T(8,128)(2,1)S(1)}, bf16[2,128,128]{2,1,0:T(8,128)(2,1)S(1)}, u32[]{:S(2)}, u32[]{:S(2)}) collective-permute-start(bf16[2,128,128]{2,1,0:T(8,128)(2,1)S(1)} %get-tuple-element.328), channel_id=1, source_target_pairs={{0,16},{16,32},{32,48},{48,64},{64,80},{80,96},{96,112},{112,128},... | collective-permute-start | bytes 196616 | tf_op jit(solution)/shard_map/while/body/eval_jaxpr/ppermute | solution.py:14
  140.2 5.3 %collective-permute-start = (bf16[2,128,128]{2,1,0:T(8,128)(2,1)S(1)}, bf16[2,128,128]{2,1,0:T(8,128)(2,1)S(1)}, u32[]{:S(2)}, u32[]{:S(2)}) collective-permute-start(bf16[2,128,128]{2,1,0:T(8,128)(2,1)S(1)} %get-tuple-element.328), channel_id=1, source_target_pairs={{0,16},{16,32},{32,48},{48,64},{64,80},{80,96},{96,112},{112,128},... | collective-permute-start | bytes 196616 | tf_op jit(solution)/shard_map/while/body/eval_jaxpr/ppermute | solution.py:14
  146.9 5.3 %collective-permute-start = (bf16[2,128,128]{2,1,0:T(8,128)(2,1)S(1)}, bf16[2,128,128]{2,1,0:T(8,128)(2,1)S(1)}, u32[]{:S(2)}, u32[]{:S(2)}) collective-permute-start(bf16[2,128,128]{2,1,0:T(8,128)(2,1)S(1)} %get-tuple-element.328), channel_id=1, source_target_pairs={{0,16},{16,32},{32,48},{48,64},{64,80},{80,96},{96,112},{112,128},... | collective-permute-start | bytes 196616 | tf_op jit(solution)/shard_map/while/body/eval_jaxpr/ppermute | solution.py:14
  153.7 5.3 %collective-permute-start = (bf16[2,128,128]{2,1,0:T(8,128)(2,1)S(1)}, bf16[2,128,128]{2,1,0:T(8,128)(2,1)S(1)}, u32[]{:S(2)}, u32[]{:S(2)}) collective-permute-start(bf16[2,128,128]{2,1,0:T(8,128)(2,1)S(1)} %get-tuple-element.328), channel_id=1, source_target_pairs={{0,16},{16,32},{32,48},{48,64},{64,80},{80,96},{96,112},{112,128},... | collective-permute-start | bytes 196616 | tf_op jit(solution)/shard_map/while/body/eval_jaxpr/ppermute | solution.py:14
  160.4 5.3 %collective-permute-start = (bf16[2,128,128]{2,1,0:T(8,128)(2,1)S(1)}, bf16[2,128,128]{2,1,0:T(8,128)(2,1)S(1)}, u32[]{:S(2)}, u32[]{:S(2)}) collective-permute-start(bf16[2,128,128]{2,1,0:T(8,128)(2,1)S(1)} %get-tuple-element.328), channel_id=1, source_target_pairs={{0,16},{16,32},{32,48},{48,64},{64,80},{80,96},{96,112},{112,128},... | collective-permute-start | bytes 196616 | tf_op jit(solution)/shard_map/while/body/eval_jaxpr/ppermute | solution.py:14
  167.1 5.3 %collective-permute-start = (bf16[2,128,128]{2,1,0:T(8,128)(2,1)S(1)}, bf16[2,128,128]{2,1,0:T(8,128)(2,1)S(1)}, u32[]{:S(2)}, u32[]{:S(2)}) collective-permute-start(bf16[2,128,128]{2,1,0:T(8,128)(2,1)S(1)} %get-tuple-element.328), channel_id=1, source_target_pairs={{0,16},{16,32},{32,48},{48,64},{64,80},{80,96},{96,112},{112,128},... | collective-permute-start | bytes 196616 | tf_op jit(solution)/shard_map/while/body/eval_jaxpr/ppermute | solution.py:14
  173.9 6.0 %collective-permute-start = (bf16[2,128,128]{2,1,0:T(8,128)(2,1)S(1)}, bf16[2,128,128]{2,1,0:T(8,128)(2,1)S(1)}, u32[]{:S(2)}, u32[]{:S(2)}) collective-permute-start(bf16[2,128,128]{2,1,0:T(8,128)(2,1)S(1)} %get-tuple-element.328), channel_id=1, source_target_pairs={{0,16},{16,32},{32,48},{48,64},{64,80},{80,96},{96,112},{112,128},... | collective-permute-start | bytes 196616 | tf_op jit(solution)/shard_map/while/body/eval_jaxpr/ppermute | solution.py:14
  189.9 0.7 copy-start.2
  189.9 22.0 %copy-start.5 = (u32[256]{0:T(256)S(1)}, u32[256]{0:T(256)}, u32[]{:S(2)}) copy-start(u32[256]{0:T(256)} %constant.141) | copy-start | bytes 3076
  189.9 23.3 %copy-start.1 = (s32[6,128]{1,0:T(8,128)S(1)}, s32[6,128]{1,0:T(8,128)}, u32[]{:S(2)}) copy-start(s32[6,128]{1,0:T(8,128)} %param.20) | copy-start | bytes 9220
  189.9 23.3 %copy-start = (f32[6,128]{1,0:T(8,128)S(1)}, f32[6,128]{1,0:T(8,128)}, u32[]{:S(2)}) copy-start(f32[6,128]{1,0:T(8,128)} %param.19) | copy-start | bytes 9220
  191.3 21.9 %collective-permute-start.1 = (f32[2,128,64]{2,1,0:T(8,128)S(1)}, f32[2,128,64]{2,1,0:T(8,128)S(1)}, u32[]{:S(2)}, u32[]{:S(2)}) collective-permute-start(f32[2,128,64]{2,1,0:T(8,128)S(1)} %select_bitcast_fusion.1), channel_id=1, source_target_pairs={{0,1},{1,2},{2,3},{3,4},{4,5},{5,6},{6,7},{7,8},{8,9},{9,10},{10,1... | collective-permute-start | bytes 196616 | tf_op jit(solution)/shard_map/ppermute | solution.py:25
  208.7 10.2 %collective-permute-start.2 = (f32[2,128,64]{2,1,0:T(8,128)S(1)}, f32[2,128,64]{2,1,0:T(8,128)S(1)}, u32[]{:S(2)}, u32[]{:S(2)}) collective-permute-start(f32[2,128,64]{2,1,0:T(8,128)S(1)} %select_bitcast_fusion), channel_id=1, source_target_pairs={{1,0},{2,1},{3,2},{4,3},{5,4},{6,5},{7,6},{8,7},{9,8},{10,9},{11,1... | collective-permute-start | bytes 196616 | tf_op jit(solution)/shard_map/ppermute | solution.py:27
  220.0 129.5 %copy-start.3 = (f32[128]{0:T(128)S(1)}, f32[128]{0:T(128)}, u32[]{:S(2)}) copy-start(f32[128]{0:T(128)} %param.18) | copy-start | bytes 1540
  220.0 129.5 %copy-start.4 = (f32[128]{0:T(128)S(1)}, f32[128]{0:T(128)}, u32[]{:S(2)}) copy-start(f32[128]{0:T(128)} %param.17) | copy-start | bytes 1540
Sparse Core Ops, SparseCore 0:
  190.0 158.1 all-reduce.2
where the time goes:
time: 357 us
  waiting for transfers between devices  141 us (39%)
  other arithmetic  82.2 us (23%)
  blocking collectives  62.2 us (17%)
  starting transfers between devices  23.9 us (7%)
  local copies, waits for them, and re-layouts  20.2 us (6%)
  between operations  14.4 us (4%)
  matrix products  11.8 us (3%)
    unnamed x2, waiting for transfers between devices  124 us
    convert_element_type x16, other arithmetic, kernel_table(): cosine = (scaled * jnp.cos(phase)).astype(jnp.bfloat16)  68.5 us
    all_gather x1, blocking collectives, local(): target_place = lax.all_gather(positions, 'grp', axis=1, tiled=True)  31.7 us
    all_gather x1, blocking collectives, local(): source_place = lax.all_gather(positions, 'blk', axis=1, tiled=True)  30.5 us
    ppermute x1, starting transfers between devices, with_halo(): lax.ppermute(tail, axis, [(i, (i + 1) % count) for i in range(ends)])  16.5 us
    ppermute x15, waiting for transfers between devices, from_behind(): lax.ppermute(array, axis, [(i, (i + by) % size) for i in range(size)])  11.9 us
    dot_general x16, matrix products, block_columns(): product = jnp.dot(flat, kernel, preferred_element_type=jnp.float32)  11.8 us
    while x2, local copies, waits for them, and re-layouts, local(): lax.fori_loop(1, block_count, advance, (total, section_half))  10.4 us
  transfers between devices with their start and end apart: 18, of which 17 were waited for; matrix products, arithmetic and copies ran while one was open for 20% of the time, Pallas kernels for 0%

commit v1 on v0

--- a/solution.py
+++ b/solution.py
@@ -61,7 +61,9 @@
     section_half = section_field.astype(jnp.bfloat16)
     my_index = lax.axis_index("blk")
     target_place = lax.all_gather(positions, "grp", axis=1, tiled=True)
-    source_place = lax.all_gather(positions, "blk", axis=1, tiled=True)
+    source_place = jnp.concatenate(
+        lax.all_to_all(jnp.stack([positions] * lax.axis_size("blk")), "blk", 0, 0), axis=1
+    )
     targets = target_place.shape[1]
 
     def place_of(block_index):

time: 357 us -> 336 us (0.941)
  blocking collectives: 62.2 us -> 25 us
  starting transfers between devices: 23.9 us -> 40.4 us
    all_gather x1 -> x0, blocking collectives: 30.5 us -> none  [local(): source_place = lax.all_gather(positions, 'blk', axis=1, tiled=True)]
    all_to_all x0 -> x1, starting transfers between devices: none -> 10.1 us  [local(): lax.all_to_all(jnp.stack([positions] * lax.axis_size('blk')), 'blk', 0, 0)]
    ppermute x15, starting transfers between devices: 4.14 us -> 14.1 us  [from_behind(): lax.ppermute(array, axis, [(i, (i + by) % size) for i in range(size)])]
    all_gather x1, blocking collectives: 31.7 us -> 25 us  [local(): target_place = lax.all_gather(positions, 'grp', axis=1, tiled=True)]
    ppermute x15, waiting for transfers between devices: 11.9 us -> 5.66 us  [from_behind(): lax.ppermute(array, axis, [(i, (i + by) % size) for i in range(size)])]
    unnamed x2, waiting for transfers between devices: 124 us -> 130 us
  transfers between devices with their start and end apart: 18 -> 19, of which waited for: 17 -> 11; matrix products, arithmetic and copies ran while one was open for 20% -> 22% of each run, Pallas kernels for 0% -> 0%
where the time goes in v1:
time: 336 us
  waiting for transfers between devices  139 us (41%)
  other arithmetic  82.2 us (24%)
  starting transfers between devices  40.4 us (12%)
  blocking collectives  25 us (7%)
  local copies, waits for them, and re-layouts  21.5 us (6%)
  between operations  14.4 us (4%)
  matrix products  11.8 us (4%)
    unnamed x2, waiting for transfers between devices  130 us
    convert_element_type x16, other arithmetic, kernel_table(): cosine = (scaled * jnp.cos(phase)).astype(jnp.bfloat16)  68.5 us
    all_gather x1, blocking collectives, local(): target_place = lax.all_gather(positions, 'grp', axis=1, tiled=True)  25 us
    ppermute x15, starting transfers between devices, from_behind(): lax.ppermute(array, axis, [(i, (i + by) % size) for i in range(size)])  14.1 us
    ppermute x1, starting transfers between devices, with_halo(): lax.ppermute(tail, axis, [(i, (i + 1) % count) for i in range(ends)])  13.4 us
    dot_general x16, matrix products, block_columns(): product = jnp.dot(flat, kernel, preferred_element_type=jnp.float32)  11.8 us
    while x2, local copies, waits for them, and re-layouts, local(): lax.fori_loop(1, block_count, advance, (total, section_half))  10.4 us
    all_to_all x1, starting transfers between devices, local(): lax.all_to_all(jnp.stack([positions] * lax.axis_size('blk')), 'blk', 0, 0)  10.1 us
  transfers between devices with their start and end apart: 19, of which 11 were waited for; matrix products, arithmetic and copies ran while one was open for 22% of the time, Pallas kernels for 0%

profile of v1, /device:TPU:1, one launch (start us, length us, event | category | flops | bytes accessed | tf_op | source)
XLA Modules:
  0.0 335.5 jit_solution(1115007951686455971)
XLA Ops:
  6.5 1.3 stack.63
  7.8 10.1 %all-to-all-start = ((f32[16,2,128]{2,1,0:T(2,128)}), f32[16,2,128]{2,1,0:T(2,128)S(1)}, u32[]{:S(2)}, u32[]{:S(2)}) async-start(f32[16,2,128]{2,1,0:T(2,128)} %stack.63), calls=%async_computation | async-start | bytes 32768 | tf_op jit(solution)/shard_map/all_to_all | solution.py:65
  18.0 25.0 %all_gather.3 = f32[2,2048]{1,0:T(2,128)S(1)} all-gather(f32[2,128]{1,0:T(2,128)} %param.16), channel_id=1, replica_groups=mesh['blk'=16,'grp'=16] {'grp'}, dimensions={1}, use_global_device_ids=true | all-gather | bytes 17408 | tf_op jit(solution)/shard_map/all_gather | solution.py:63
  43.1 1.0 fusion.18
  44.1 4.3 %multiply_convert_fusion.3 = (bf16[128,2048]{1,0:T(8,128)(2,1)S(1)}, bf16[128,2048]{1,0:T(8,128)(2,1)S(1)}) fusion(f32[128]{0:T(128)S(1)} %get-tuple-element.252, f32[2048]{0:T(1024)S(1)} %bitcast.121, f32[128]{0:T(128)S(1)} %get-tuple-element.251, f32[2048]{0:T(1024)S(1)} %bitcast.120), kind=kLoop, calls=%fused_computation.34 | loop fusion | flops 2621440 | bytes 1065984 | tf_op jit(solution)/shard_map/convert_element_type | solution.py:38
  48.4 0.7 fusion.8
  49.4 1.6 pad_maximum_fusion
  50.9 1.9 copy.23
  52.9 106.5 %while.17 = (s32[]{:T(128)}, f32[2,128,2048]{1,2,0:T(8,128)S(1)}, bf16[2,128,128]{2,1,0:T(8,128)(2,1)S(1)}, f32[2,2048]{1,0:T(2,128)S(1)}, s32[]{:T(128)}, /*ind...) while((s32[]{:T(128)}, f32[2,128,2048]{1,2,0:T(8,128)S(1)}, ...), condition=%wide.region_1.2_spmd, body=%wide.region_0.1_spmd.sunk | while | flops 274726944 | bytes 19387720 | solution.py:85
  52.9 1.1 collective-permute-start
  54.0 4.3 %multiply_convert_fusion.5 = (bf16[128,2048]{1,0:T(8,128)(2,1)S(1)}, bf16[128,2048]{1,0:T(8,128)(2,1)S(1)}) fusion(f32[128]{0:T(128)S(1)} %get-tuple-element.306, f32[2048]{0:T(1024)S(1)} %bitcast.118, f32[128]{0:T(128)S(1)} %get-tuple-element.308, f32[2048]{0:T(1024)S(1)} %bitcast.117), kind=kLoop, calls=%fused_computation.18.clone.1 | loop fusion | flops 2621440 | bytes 1065984 | tf_op jit(solution)/shard_map/while/body/eval_jaxpr/convert_element_type | solution.py:38
  58.6 0.7 convolution_bitcast_fusion.2
  60.0 1.6 collective-permute-start
  61.6 4.3 %multiply_convert_fusion.5 = (bf16[128,2048]{1,0:T(8,128)(2,1)S(1)}, bf16[128,2048]{1,0:T(8,128)(2,1)S(1)}) fusion(f32[128]{0:T(128)S(1)} %get-tuple-element.306, f32[2048]{0:T(1024)S(1)} %bitcast.118, f32[128]{0:T(128)S(1)} %get-tuple-element.308, f32[2048]{0:T(1024)S(1)} %bitcast.117), kind=kLoop, calls=%fused_computation.18.clone.1 | loop fusion | flops 2621440 | bytes 1065984 | tf_op jit(solution)/shard_map/while/body/eval_jaxpr/convert_element_type | solution.py:38
  65.9 0.7 convolution_bitcast_fusion.2
  68.1 4.3 %multiply_convert_fusion.5 = (bf16[128,2048]{1,0:T(8,128)(2,1)S(1)}, bf16[128,2048]{1,0:T(8,128)(2,1)S(1)}) fusion(f32[128]{0:T(128)S(1)} %get-tuple-element.306, f32[2048]{0:T(1024)S(1)} %bitcast.118, f32[128]{0:T(128)S(1)} %get-tuple-element.308, f32[2048]{0:T(1024)S(1)} %bitcast.117), kind=kLoop, calls=%fused_computation.18.clone.1 | loop fusion | flops 2621440 | bytes 1065984 | tf_op jit(solution)/shard_map/while/body/eval_jaxpr/convert_element_type | solution.py:38
  72.7 0.7 convolution_bitcast_fusion.2
  74.1 1.6 collective-permute-start
  75.7 4.3 %multiply_convert_fusion.5 = (bf16[128,2048]{1,0:T(8,128)(2,1)S(1)}, bf16[128,2048]{1,0:T(8,128)(2,1)S(1)}) fusion(f32[128]{0:T(128)S(1)} %get-tuple-element.306, f32[2048]{0:T(1024)S(1)} %bitcast.118, f32[128]{0:T(128)S(1)} %get-tuple-element.308, f32[2048]{0:T(1024)S(1)} %bitcast.117), kind=kLoop, calls=%fused_computation.18.clone.1 | loop fusion | flops 2621440 | bytes 1065984 | tf_op jit(solution)/shard_map/while/body/eval_jaxpr/convert_element_type | solution.py:38
  80.0 0.7 convolution_bitcast_fusion.2
  82.1 4.3 %multiply_convert_fusion.5 = (bf16[128,2048]{1,0:T(8,128)(2,1)S(1)}, bf16[128,2048]{1,0:T(8,128)(2,1)S(1)}) fusion(f32[128]{0:T(128)S(1)} %get-tuple-element.306, f32[2048]{0:T(1024)S(1)} %bitcast.118, f32[128]{0:T(128)S(1)} %get-tuple-element.308, f32[2048]{0:T(1024)S(1)} %bitcast.117), kind=kLoop, calls=%fused_computation.18.clone.1 | loop fusion | flops 2621440 | bytes 1065984 | tf_op jit(solution)/shard_map/while/body/eval_jaxpr/convert_element_type | solution.py:38
  86.8 0.7 convolution_bitcast_fusion.2
  88.2 1.5 collective-permute-start
  89.8 4.3 %multiply_convert_fusion.5 = (bf16[128,2048]{1,0:T(8,128)(2,1)S(1)}, bf16[128,2048]{1,0:T(8,128)(2,1)S(1)}) fusion(f32[128]{0:T(128)S(1)} %get-tuple-element.306, f32[2048]{0:T(1024)S(1)} %bitcast.118, f32[128]{0:T(128)S(1)} %get-tuple-element.308, f32[2048]{0:T(1024)S(1)} %bitcast.117), kind=kLoop, calls=%fused_computation.18.clone.1 | loop fusion | flops 2621440 | bytes 1065984 | tf_op jit(solution)/shard_map/while/body/eval_jaxpr/convert_element_type | solution.py:38
  94.1 0.7 convolution_bitcast_fusion.2
  96.2 4.3 %multiply_convert_fusion.5 = (bf16[128,2048]{1,0:T(8,128)(2,1)S(1)}, bf16[128,2048]{1,0:T(8,128)(2,1)S(1)}) fusion(f32[128]{0:T(128)S(1)} %get-tuple-element.306, f32[2048]{0:T(1024)S(1)} %bitcast.118, f32[128]{0:T(128)S(1)} %get-tuple-element.308, f32[2048]{0:T(1024)S(1)} %bitcast.117), kind=kLoop, calls=%fused_computation.18.clone.1 | loop fusion | flops 2621440 | bytes 1065984 | tf_op jit(solution)/shard_map/while/body/eval_jaxpr/convert_element_type | solution.py:38
  100.8 0.7 convolution_bitcast_fusion.2
  102.3 2.7 collective-permute-start
  105.0 4.3 %multiply_convert_fusion.5 = (bf16[128,2048]{1,0:T(8,128)(2,1)S(1)}, bf16[128,2048]{1,0:T(8,128)(2,1)S(1)}) fusion(f32[128]{0:T(128)S(1)} %get-tuple-element.306, f32[2048]{0:T(1024)S(1)} %bitcast.118, f32[128]{0:T(128)S(1)} %get-tuple-element.308, f32[2048]{0:T(1024)S(1)} %bitcast.117), kind=kLoop, calls=%fused_computation.18.clone.1 | loop fusion | flops 2621440 | bytes 1065984 | tf_op jit(solution)/shard_map/while/body/eval_jaxpr/convert_element_type | solution.py:38
  109.3 0.7 convolution_bitcast_fusion.2
  110.8 1.4 collective-permute-start
  112.2 4.3 %multiply_convert_fusion.5 = (bf16[128,2048]{1,0:T(8,128)(2,1)S(1)}, bf16[128,2048]{1,0:T(8,128)(2,1)S(1)}) fusion(f32[128]{0:T(128)S(1)} %get-tuple-element.306, f32[2048]{0:T(1024)S(1)} %bitcast.118, f32[128]{0:T(128)S(1)} %get-tuple-element.308, f32[2048]{0:T(1024)S(1)} %bitcast.117), kind=kLoop, calls=%fused_computation.18.clone.1 | loop fusion | flops 2621440 | bytes 1065984 | tf_op jit(solution)/shard_map/while/body/eval_jaxpr/convert_element_type | solution.py:38
  116.5 0.7 convolution_bitcast_fusion.2
  117.9 1.0 collective-permute-start
  118.9 4.3 %multiply_convert_fusion.5 = (bf16[128,2048]{1,0:T(8,128)(2,1)S(1)}, bf16[128,2048]{1,0:T(8,128)(2,1)S(1)}) fusion(f32[128]{0:T(128)S(1)} %get-tuple-element.306, f32[2048]{0:T(1024)S(1)} %bitcast.118, f32[128]{0:T(128)S(1)} %get-tuple-element.308, f32[2048]{0:T(1024)S(1)} %bitcast.117), kind=kLoop, calls=%fused_computation.18.clone.1 | loop fusion | flops 2621440 | bytes 1065984 | tf_op jit(solution)/shard_map/while/body/eval_jaxpr/convert_element_type | solution.py:38
  123.2 0.7 convolution_bitcast_fusion.2
  124.7 1.0 collective-permute-start
  125.7 4.3 %multiply_convert_fusion.5 = (bf16[128,2048]{1,0:T(8,128)(2,1)S(1)}, bf16[128,2048]{1,0:T(8,128)(2,1)S(1)}) fusion(f32[128]{0:T(128)S(1)} %get-tuple-element.306, f32[2048]{0:T(1024)S(1)} %bitcast.118, f32[128]{0:T(128)S(1)} %get-tuple-element.308, f32[2048]{0:T(1024)S(1)} %bitcast.117), kind=kLoop, calls=%fused_computation.18.clone.1 | loop fusion | flops 2621440 | bytes 1065984 | tf_op jit(solution)/shard_map/while/body/eval_jaxpr/convert_element_type | solution.py:38
  129.9 1.0 collective-permute-done
  130.9 0.7 convolution_bitcast_fusion.2
  132.5 4.3 %multiply_convert_fusion.5 = (bf16[128,2048]{1,0:T(8,128)(2,1)S(1)}, bf16[128,2048]{1,0:T(8,128)(2,1)S(1)}) fusion(f32[128]{0:T(128)S(1)} %get-tuple-element.306, f32[2048]{0:T(1024)S(1)} %bitcast.118, f32[128]{0:T(128)S(1)} %get-tuple-element.308, f32[2048]{0:T(1024)S(1)} %bitcast.117), kind=kLoop, calls=%fused_computation.18.clone.1 | loop fusion | flops 2621440 | bytes 1065984 | tf_op jit(solution)/shard_map/while/body/eval_jaxpr/convert_element_type | solution.py:38
  136.8 0.8 collective-permute-done
  137.7 0.7 convolution_bitcast_fusion.2
  139.3 4.3 %multiply_convert_fusion.5 = (bf16[128,2048]{1,0:T(8,128)(2,1)S(1)}, bf16[128,2048]{1,0:T(8,128)(2,1)S(1)}) fusion(f32[128]{0:T(128)S(1)} %get-tuple-element.306, f32[2048]{0:T(1024)S(1)} %bitcast.118, f32[128]{0:T(128)S(1)} %get-tuple-element.308, f32[2048]{0:T(1024)S(1)} %bitcast.117), kind=kLoop, calls=%fused_computation.18.clone.1 | loop fusion | flops 2621440 | bytes 1065984 | tf_op jit(solution)/shard_map/while/body/eval_jaxpr/convert_element_type | solution.py:38
  143.6 0.8 collective-permute-done
  144.4 0.7 convolution_bitcast_fusion.2
  146.0 4.3 %multiply_convert_fusion.5 = (bf16[128,2048]{1,0:T(8,128)(2,1)S(1)}, bf16[128,2048]{1,0:T(8,128)(2,1)S(1)}) fusion(f32[128]{0:T(128)S(1)} %get-tuple-element.306, f32[2048]{0:T(1024)S(1)} %bitcast.118, f32[128]{0:T(128)S(1)} %get-tuple-element.308, f32[2048]{0:T(1024)S(1)} %bitcast.117), kind=kLoop, calls=%fused_computation.18.clone.1 | loop fusion | flops 2621440 | bytes 1065984 | tf_op jit(solution)/shard_map/while/body/eval_jaxpr/convert_element_type | solution.py:38
  150.3 0.8 collective-permute-done
  151.1 0.7 convolution_bitcast_fusion.2
  152.8 4.3 %multiply_convert_fusion.5 = (bf16[128,2048]{1,0:T(8,128)(2,1)S(1)}, bf16[128,2048]{1,0:T(8,128)(2,1)S(1)}) fusion(f32[128]{0:T(128)S(1)} %get-tuple-element.306, f32[2048]{0:T(1024)S(1)} %bitcast.118, f32[128]{0:T(128)S(1)} %get-tuple-element.308, f32[2048]{0:T(1024)S(1)} %bitcast.117), kind=kLoop, calls=%fused_computation.18.clone.1 | loop fusion | flops 2621440 | bytes 1065984 | tf_op jit(solution)/shard_map/while/body/eval_jaxpr/convert_element_type | solution.py:38
  157.0 0.8 collective-permute-done
  157.9 0.7 convolution_bitcast_fusion.2
  159.3 8.5 %copy.24 = f32[2,128,2048]{1,0,2:T(2,128)} copy(f32[2,128,2048]{1,2,0:T(8,128)S(1)} %get-tuple-element.162) | data formatting | bytes 4194304 | tf_op jit(solution)/shard_map/while | solution.py:85
  169.4 13.4 %collective-permute-start.1 = (f32[2,128,64]{2,1,0:T(8,128)S(1)}, f32[2,128,64]{2,1,0:T(8,128)S(1)}, u32[]{:S(2)}, u32[]{:S(2)}) collective-permute-start(f32[2,128,64]{2,1,0:T(8,128)S(1)} %select_bitcast_fusion.1), channel_id=1, source_target_pairs={{0,1},{1,2},{2,3},{3,4},{4,5},{5,6},{6,7},{7,8},{8,9},{9,10},{10,1... | collective-permute-start | bytes 196616 | tf_op jit(solution)/shard_map/ppermute | solution.py:25
  183.6 2.7 collective-permute-start.2
  187.6 3.8 %collective-permute-done.2 = f32[2,128,64]{2,1,0:T(8,128)S(1)} collective-permute-done((f32[2,128,64]{2,1,0:T(8,128)S(1)}, f32[2,128,64]{2,1,0:T(8,128)S(1)}, u32[]{:S(2)}, u32[]{:S(2)}) %collective-permute-start.2) | collective-permute-done | bytes 65568 | tf_op jit(solution)/shard_map/ppermute | solution.py:27
  191.7 0.7 gather_fusion.2
  192.5 0.7 gather_fusion.3
  193.4 0.7 gather_fusion.4
  194.2 0.7 gather_fusion.5
  195.1 0.7 gather_fusion.6
  196.0 0.8 gather_fusion.7
  196.9 129.8 %all-reduce.3.cloned.1.call-done = f32[2,128,2048]{1,0,2:T(2,128)} async-done(((f32[2,128,2048]{1,0,2:T(2,128)}), f32[2,128,2048]{1,0,2:T(2,128)}) %all-reduce.3.cloned.1.call-update) | async-done | bytes 2097168
  326.7 1.1 constant_dynamic-slice_fusion.1
  (156 shorter events, 18.9 us)
Async XLA Ops:
  7.8 36.3 %all-to-all-start = ((f32[16,2,128]{2,1,0:T(2,128)}), f32[16,2,128]{2,1,0:T(2,128)S(1)}, u32[]{:S(2)}, u32[]{:S(2)}) async-start(f32[16,2,128]{2,1,0:T(2,128)} %stack.63), calls=%async_computation | async-start | bytes 32768 | tf_op jit(solution)/shard_map/all_to_all | solution.py:65
  18.0 308.7 %all-reduce.3.cloned.1.call-start = ((), (), s32[]{:S(2)}) async-start(), calls=%async_computation.1 | async-start | bytes 4194304
  52.9 5.7 %collective-permute-start = (bf16[2,128,128]{2,1,0:T(8,128)(2,1)S(1)}, bf16[2,128,128]{2,1,0:T(8,128)(2,1)S(1)}, u32[]{:S(2)}, u32[]{:S(2)}) collective-permute-start(bf16[2,128,128]{2,1,0:T(8,128)(2,1)S(1)} %get-tuple-element.328), channel_id=1, source_target_pairs={{0,16},{16,32},{32,48},{48,64},{64,80},{80,96},{96,112},{112,128},... | collective-permute-start | bytes 196616 | tf_op jit(solution)/shard_map/while/body/eval_jaxpr/ppermute | solution.py:14
  60.0 5.9 %collective-permute-start = (bf16[2,128,128]{2,1,0:T(8,128)(2,1)S(1)}, bf16[2,128,128]{2,1,0:T(8,128)(2,1)S(1)}, u32[]{:S(2)}, u32[]{:S(2)}) collective-permute-start(bf16[2,128,128]{2,1,0:T(8,128)(2,1)S(1)} %get-tuple-element.328), channel_id=1, source_target_pairs={{0,16},{16,32},{32,48},{48,64},{64,80},{80,96},{96,112},{112,128},... | collective-permute-start | bytes 196616 | tf_op jit(solution)/shard_map/while/body/eval_jaxpr/ppermute | solution.py:14
  67.4 5.3 %collective-permute-start = (bf16[2,128,128]{2,1,0:T(8,128)(2,1)S(1)}, bf16[2,128,128]{2,1,0:T(8,128)(2,1)S(1)}, u32[]{:S(2)}, u32[]{:S(2)}) collective-permute-start(bf16[2,128,128]{2,1,0:T(8,128)(2,1)S(1)} %get-tuple-element.328), channel_id=1, source_target_pairs={{0,16},{16,32},{32,48},{48,64},{64,80},{80,96},{96,112},{112,128},... | collective-permute-start | bytes 196616 | tf_op jit(solution)/shard_map/while/body/eval_jaxpr/ppermute | solution.py:14
  74.1 5.9 %collective-permute-start = (bf16[2,128,128]{2,1,0:T(8,128)(2,1)S(1)}, bf16[2,128,128]{2,1,0:T(8,128)(2,1)S(1)}, u32[]{:S(2)}, u32[]{:S(2)}) collective-permute-start(bf16[2,128,128]{2,1,0:T(8,128)(2,1)S(1)} %get-tuple-element.328), channel_id=1, source_target_pairs={{0,16},{16,32},{32,48},{48,64},{64,80},{80,96},{96,112},{112,128},... | collective-permute-start | bytes 196616 | tf_op jit(solution)/shard_map/while/body/eval_jaxpr/ppermute | solution.py:14
  81.4 5.3 %collective-permute-start = (bf16[2,128,128]{2,1,0:T(8,128)(2,1)S(1)}, bf16[2,128,128]{2,1,0:T(8,128)(2,1)S(1)}, u32[]{:S(2)}, u32[]{:S(2)}) collective-permute-start(bf16[2,128,128]{2,1,0:T(8,128)(2,1)S(1)} %get-tuple-element.328), channel_id=1, source_target_pairs={{0,16},{16,32},{32,48},{48,64},{64,80},{80,96},{96,112},{112,128},... | collective-permute-start | bytes 196616 | tf_op jit(solution)/shard_map/while/body/eval_jaxpr/ppermute | solution.py:14
  88.2 5.9 %collective-permute-start = (bf16[2,128,128]{2,1,0:T(8,128)(2,1)S(1)}, bf16[2,128,128]{2,1,0:T(8,128)(2,1)S(1)}, u32[]{:S(2)}, u32[]{:S(2)}) collective-permute-start(bf16[2,128,128]{2,1,0:T(8,128)(2,1)S(1)} %get-tuple-element.328), channel_id=1, source_target_pairs={{0,16},{16,32},{32,48},{48,64},{64,80},{80,96},{96,112},{112,128},... | collective-permute-start | bytes 196616 | tf_op jit(solution)/shard_map/while/body/eval_jaxpr/ppermute | solution.py:14
  95.5 5.3 %collective-permute-start = (bf16[2,128,128]{2,1,0:T(8,128)(2,1)S(1)}, bf16[2,128,128]{2,1,0:T(8,128)(2,1)S(1)}, u32[]{:S(2)}, u32[]{:S(2)}) collective-permute-start(bf16[2,128,128]{2,1,0:T(8,128)(2,1)S(1)} %get-tuple-element.328), channel_id=1, source_target_pairs={{0,16},{16,32},{32,48},{48,64},{64,80},{80,96},{96,112},{112,128},... | collective-permute-start | bytes 196616 | tf_op jit(solution)/shard_map/while/body/eval_jaxpr/ppermute | solution.py:14
  102.3 7.1 %collective-permute-start = (bf16[2,128,128]{2,1,0:T(8,128)(2,1)S(1)}, bf16[2,128,128]{2,1,0:T(8,128)(2,1)S(1)}, u32[]{:S(2)}, u32[]{:S(2)}) collective-permute-start(bf16[2,128,128]{2,1,0:T(8,128)(2,1)S(1)} %get-tuple-element.328), channel_id=1, source_target_pairs={{0,16},{16,32},{32,48},{48,64},{64,80},{80,96},{96,112},{112,128},... | collective-permute-start | bytes 196616 | tf_op jit(solution)/shard_map/while/body/eval_jaxpr/ppermute | solution.py:14
  110.8 5.7 %collective-permute-start = (bf16[2,128,128]{2,1,0:T(8,128)(2,1)S(1)}, bf16[2,128,128]{2,1,0:T(8,128)(2,1)S(1)}, u32[]{:S(2)}, u32[]{:S(2)}) collective-permute-start(bf16[2,128,128]{2,1,0:T(8,128)(2,1)S(1)} %get-tuple-element.328), channel_id=1, source_target_pairs={{0,16},{16,32},{32,48},{48,64},{64,80},{80,96},{96,112},{112,128},... | collective-permute-start | bytes 196616 | tf_op jit(solution)/shard_map/while/body/eval_jaxpr/ppermute | solution.py:14
  117.9 5.3 %collective-permute-start = (bf16[2,128,128]{2,1,0:T(8,128)(2,1)S(1)}, bf16[2,128,128]{2,1,0:T(8,128)(2,1)S(1)}, u32[]{:S(2)}, u32[]{:S(2)}) collective-permute-start(bf16[2,128,128]{2,1,0:T(8,128)(2,1)S(1)} %get-tuple-element.328), channel_id=1, source_target_pairs={{0,16},{16,32},{32,48},{48,64},{64,80},{80,96},{96,112},{112,128},... | collective-permute-start | bytes 196616 | tf_op jit(solution)/shard_map/while/body/eval_jaxpr/ppermute | solution.py:14
  124.7 6.3 %collective-permute-start = (bf16[2,128,128]{2,1,0:T(8,128)(2,1)S(1)}, bf16[2,128,128]{2,1,0:T(8,128)(2,1)S(1)}, u32[]{:S(2)}, u32[]{:S(2)}) collective-permute-start(bf16[2,128,128]{2,1,0:T(8,128)(2,1)S(1)} %get-tuple-element.328), channel_id=1, source_target_pairs={{0,16},{16,32},{32,48},{48,64},{64,80},{80,96},{96,112},{112,128},... | collective-permute-start | bytes 196616 | tf_op jit(solution)/shard_map/while/body/eval_jaxpr/ppermute | solution.py:14
  132.4 5.3 %collective-permute-start = (bf16[2,128,128]{2,1,0:T(8,128)(2,1)S(1)}, bf16[2,128,128]{2,1,0:T(8,128)(2,1)S(1)}, u32[]{:S(2)}, u32[]{:S(2)}) collective-permute-start(bf16[2,128,128]{2,1,0:T(8,128)(2,1)S(1)} %get-tuple-element.328), channel_id=1, source_target_pairs={{0,16},{16,32},{32,48},{48,64},{64,80},{80,96},{96,112},{112,128},... | collective-permute-start | bytes 196616 | tf_op jit(solution)/shard_map/while/body/eval_jaxpr/ppermute | solution.py:14
  139.1 5.3 %collective-permute-start = (bf16[2,128,128]{2,1,0:T(8,128)(2,1)S(1)}, bf16[2,128,128]{2,1,0:T(8,128)(2,1)S(1)}, u32[]{:S(2)}, u32[]{:S(2)}) collective-permute-start(bf16[2,128,128]{2,1,0:T(8,128)(2,1)S(1)} %get-tuple-element.328), channel_id=1, source_target_pairs={{0,16},{16,32},{32,48},{48,64},{64,80},{80,96},{96,112},{112,128},... | collective-permute-start | bytes 196616 | tf_op jit(solution)/shard_map/while/body/eval_jaxpr/ppermute | solution.py:14
  145.8 5.3 %collective-permute-start = (bf16[2,128,128]{2,1,0:T(8,128)(2,1)S(1)}, bf16[2,128,128]{2,1,0:T(8,128)(2,1)S(1)}, u32[]{:S(2)}, u32[]{:S(2)}) collective-permute-start(bf16[2,128,128]{2,1,0:T(8,128)(2,1)S(1)} %get-tuple-element.328), channel_id=1, source_target_pairs={{0,16},{16,32},{32,48},{48,64},{64,80},{80,96},{96,112},{112,128},... | collective-permute-start | bytes 196616 | tf_op jit(solution)/shard_map/while/body/eval_jaxpr/ppermute | solution.py:14
  152.6 5.3 %collective-permute-start = (bf16[2,128,128]{2,1,0:T(8,128)(2,1)S(1)}, bf16[2,128,128]{2,1,0:T(8,128)(2,1)S(1)}, u32[]{:S(2)}, u32[]{:S(2)}) collective-permute-start(bf16[2,128,128]{2,1,0:T(8,128)(2,1)S(1)} %get-tuple-element.328), channel_id=1, source_target_pairs={{0,16},{16,32},{32,48},{48,64},{64,80},{80,96},{96,112},{112,128},... | collective-permute-start | bytes 196616 | tf_op jit(solution)/shard_map/while/body/eval_jaxpr/ppermute | solution.py:14
  167.9 0.7 copy-start.2
  167.9 18.4 %copy-start.5 = (u32[256]{0:T(256)S(1)}, u32[256]{0:T(256)}, u32[]{:S(2)}) copy-start(u32[256]{0:T(256)} %constant.141) | copy-start | bytes 3076
  167.9 19.6 %copy-start.1 = (s32[6,128]{1,0:T(8,128)S(1)}, s32[6,128]{1,0:T(8,128)}, u32[]{:S(2)}) copy-start(s32[6,128]{1,0:T(8,128)} %param.20) | copy-start | bytes 9220
  167.9 19.7 %copy-start = (f32[6,128]{1,0:T(8,128)S(1)}, f32[6,128]{1,0:T(8,128)}, u32[]{:S(2)}) copy-start(f32[6,128]{1,0:T(8,128)} %param.19) | copy-start | bytes 9220
  169.4 18.3 %collective-permute-start.1 = (f32[2,128,64]{2,1,0:T(8,128)S(1)}, f32[2,128,64]{2,1,0:T(8,128)S(1)}, u32[]{:S(2)}, u32[]{:S(2)}) collective-permute-start(f32[2,128,64]{2,1,0:T(8,128)S(1)} %select_bitcast_fusion.1), channel_id=1, source_target_pairs={{0,1},{1,2},{2,3},{3,4},{4,5},{5,6},{6,7},{7,8},{8,9},{9,10},{10,1... | collective-permute-start | bytes 196616 | tf_op jit(solution)/shard_map/ppermute | solution.py:25
  183.6 7.8 %collective-permute-start.2 = (f32[2,128,64]{2,1,0:T(8,128)S(1)}, f32[2,128,64]{2,1,0:T(8,128)S(1)}, u32[]{:S(2)}, u32[]{:S(2)}) collective-permute-start(f32[2,128,64]{2,1,0:T(8,128)S(1)} %select_bitcast_fusion), channel_id=1, source_target_pairs={{1,0},{2,1},{3,2},{4,3},{5,4},{6,5},{7,6},{8,7},{9,8},{10,9},{11,1... | collective-permute-start | bytes 196616 | tf_op jit(solution)/shard_map/ppermute | solution.py:27
  192.5 135.5 %copy-start.3 = (f32[128]{0:T(128)S(1)}, f32[128]{0:T(128)}, u32[]{:S(2)}) copy-start(f32[128]{0:T(128)} %param.18) | copy-start | bytes 1540
  192.5 135.5 %copy-start.4 = (f32[128]{0:T(128)S(1)}, f32[128]{0:T(128)}, u32[]{:S(2)}) copy-start(f32[128]{0:T(128)} %param.17) | copy-start | bytes 1540
Sparse Core Ops, SparseCore 0:
  168.0 158.5 all-reduce.2
